TPU v7x, 32 devices: a whole 2x2x4 slice. The times are simulated.
32 devices in a mesh: gx: 2 (over y), gy: 4 (over x, core), gz: 4 (over z).
Axes of the slice: x: 2, y: 2, z: 4, core: 2. Of those that a mesh axis runs over, the one named last changes fastest.
Arguments:
- noise_vectors: bfloat16 [9, 4096, 128], P(None, ('gx', 'gy', 'gz')), may hold values from -6 to 6
- hamiltonian: bfloat16 [15, 9, 9, 4096], P(None, None, None, ('gx', 'gy', 'gz')), may hold values from -0.25 to 0.25
- derivative: bfloat16 [3, 15, 9, 9, 4096], P(None, None, None, None, ('gx', 'gy', 'gz')), may hold values from -0.625 to 0.625
- neighbours: int32 [4096, 15], P(('gx', 'gy', 'gz')), may hold values from 0 to 4095, as said below
- coefficients: float32 [4], replicated, may hold values from -1 to 1
Outputs:
- weighted: float32 [9, 4096, 128], P(None, ('gx', 'gy', 'gz'))
- forces: float32 [3, 4096], P(None, ('gx', 'gy', 'gz'))
Inputs may be any that keep to these rules, and one draw needn't show every extreme that they name: `neighbours`: slot 0 of every atom's list is the atom itself; the other 14 slots name distinct other atoms whose cells differ from its own by at most one along each dimension, periodically on the grid of 8 x 16 x 16 cells with two atoms a cell. Atom ids run over domains in the order gx, gy, gz, each domain holding 128 atoms numbered by (atom of the cell, first, second, third cell index within the domain).
All inputs are finite; a program needn't handle non-finite values.
Results may differ from a plain program's by a relative error of at most 0.0003.
Values may be sent and summed in bfloat16 or wider, within the bound.
A program may use at most 128 MiB of HBM per device.

v0:
```python
import functools

import jax
import jax.numpy as jnp
import numpy as np
from jax import lax
from jax.experimental import pallas as pl
from jax.experimental.pallas import tpu as pltpu
from jax.sharding import PartitionSpec as P

MESH = pl.DeviceIdType.MESH
CX = 4
CY = 4
CZ = 4
NEIGH = 15
ORB = 9
LANES = 128
GHOST = 384
EXT = LANES + GHOST
WIDE = ORB * LANES


def ghost_segments():
    found = []
    for dx in (-1, 0, 1):
        for dy in (-1, 0, 1):
            for dz in (-1, 0, 1):
                if (dx, dy, dz) != (0, 0, 0):
                    count = 2 * 4 ** ((dx == 0) + (dy == 0) + (dz == 0))
                    found.append(((dx, dy, dz), count))
    found.sort(key=lambda item: -item[1])
    placed = []
    row = 0
    for direction, count in found:
        rows = max(count, 8)
        placed.append((direction, row, rows))
        row += rows
    return placed, row


SEGMENTS, USED = ghost_segments()
COPIES = len(SEGMENTS)


def picking_matrix():
    picks = np.zeros((GHOST, LANES), np.float32)
    for (dx, dy, dz), first, _ in SEGMENTS:
        row = first
        for basis in range(2):
            for x in range(CX) if dx == 0 else ((0,) if dx > 0 else (CX - 1,)):
                for y in range(CY) if dy == 0 else ((0,) if dy > 0 else (CY - 1,)):
                    for z in range(CZ) if dz == 0 else ((0,) if dz > 0 else (CZ - 1,)):
                        picks[row, ((basis * CX + x) * CY + y) * CZ + z] = 1.0
                        row += 1
    return picks


def dot(a, b):
    return jnp.dot(a, b, preferred_element_type=jnp.float32)


def dot_t(a, b):
    return lax.dot_general(a, b, (((1,), (1,)), ((), ())), preferred_element_type=jnp.float32)


def halves(x):
    high = x.astype(jnp.bfloat16)
    return high, (x - high.astype(jnp.float32)).astype(jnp.bfloat16)


def kernel(
    sizes,
    noise,
    ham,
    deriv,
    index,
    coef,
    picks,
    w_out,
    f_out,
    ht_own,
    ht_ghost,
    onehot,
    ext_own,
    ext_ghost,
    noise_ext,
    gathered,
    chain,
    res,
    acc,
    sbuf,
    rbuf,
    fsend,
    frecv,
    pairs,
    dens,
    send_sem,
    recv_sem,
):
    f32 = jnp.float32
    bf16 = jnp.bfloat16
    here = [lax.axis_index(name) for name in ("gx", "gy", "gz")]

    def shifted(direction, sign):
        return tuple(
            lax.rem(me + size + sign * d, size) for me, size, d in zip(here, sizes, direction)
        )

    barrier = pltpu.get_barrier_semaphore()
    for direction, _, _ in SEGMENTS:
        pl.semaphore_signal(barrier, inc=1, device_id=shifted(direction, -1), device_id_type=MESH)
    for step in range(3):
        rbuf[step, :, USED:GHOST] = jnp.zeros((ORB, GHOST - USED, LANES), f32)
    frecv[USED:GHOST] = jnp.zeros((GHOST - USED, LANES), f32)
    for b in range(ORB):
        sbuf[0, b] = dot(picks[...], noise[b])
    pl.semaphore_wait(barrier, COPIES)

    def copies(step):
        made = []
        for at, (direction, first, rows) in enumerate(SEGMENTS):
            made.append(
                pltpu.make_async_remote_copy(
                    src_ref=sbuf.at[step, :, pl.ds(first, rows), :],
                    dst_ref=rbuf.at[step, :, pl.ds(first, rows), :],
                    send_sem=send_sem.at[step, at],
                    recv_sem=recv_sem.at[step, at],
                    device_id=shifted(direction, -1),
                    device_id_type=MESH,
                )
            )
        return made

    flying = [copies(step) for step in range(3)]
    for copy in flying[0]:
        copy.start()

    for b in range(ORB):
        turned = noise[b].astype(f32).T
        chain[0, :, b * LANES : (b + 1) * LANES] = turned
        ext_own[0:LANES, b * LANES : (b + 1) * LANES] = turned.astype(bf16)
        noise_ext[b * LANES : (b + 1) * LANES, 0:LANES] = turned.astype(bf16)

    @pl.loop(0, EXT // LANES)
    def _(part):
        first = pl.multiple_of(part * LANES, LANES)
        rows = lax.broadcasted_iota(jnp.int32, (LANES, LANES), 0) + first
        for m in range(NEIGH):
            same = rows == index[m : m + 1, :]
            onehot[pl.ds(first, LANES), m * LANES : (m + 1) * LANES] = jnp.where(
                same, 1.0, 0.0
            ).astype(bf16)

    def block_columns(a, first, store):
        rows = [ham[m, a].astype(f32) for m in range(NEIGH)]
        for b in range(ORB):
            total = None
            for m in range(NEIGH):
                row = jnp.broadcast_to(rows[m][b : b + 1], (16, LANES)).astype(bf16)
                hot = onehot[pl.ds(first, LANES), m * LANES : (m + 1) * LANES]
                term = hot.reshape(8, 16, LANES) * row[None]
                total = term if total is None else total + term
            store(b, total.reshape(LANES, LANES))

    @pl.loop(0, ORB)
    def _(a):
        columns = pl.ds(pl.multiple_of(a * LANES, LANES), LANES)

        def store_own(b, block):
            ht_own[b * LANES : (b + 1) * LANES, columns] = block

        block_columns(a, 0, store_own)

        @pl.loop(0, GHOST // LANES)
        def _(part):
            first = pl.multiple_of(part * LANES, LANES)

            def store_ghost(b, block):
                ht_ghost[pl.ds(b * GHOST + first, LANES), columns] = block

            block_columns(a, first + LANES, store_ghost)

    def multiply_own(rows):
        @pl.loop(0, 3)
        def _(part):
            columns = pl.ds(pl.multiple_of(part * GHOST, GHOST), GHOST)
            acc[0:rows, columns] = dot(ext_own[0:rows], ht_own[:, columns])

    def multiply_ghost(rows):
        @pl.loop(0, 3)
        def _(part):
            columns = pl.ds(pl.multiple_of(part * GHOST, GHOST), GHOST)
            acc[0:rows, columns] += dot(ext_ghost[0:rows], ht_ghost[:, columns])

    multiply_own(LANES)
    for copy in flying[0]:
        copy.wait_recv()
    for b in range(ORB):
        turned = rbuf[0, b].T.astype(bf16)
        ext_ghost[0:LANES, b * GHOST : (b + 1) * GHOST] = turned
        noise_ext[b * LANES : (b + 1) * LANES, LANES:EXT] = turned
    multiply_ghost(LANES)
    chain[1] = acc[0:LANES]
    res[...] = coef[0] * chain[0] + coef[1] * chain[1]

    def send_chain(step):
        high, low = halves(chain[step])
        ext_own[0:LANES] = high
        ext_own[LANES:] = low
        for b in range(ORB):
            cut = slice(b * LANES, (b + 1) * LANES)
            sbuf[step, b] = dot_t(picks[...], ext_own[0:LANES, cut]) + dot_t(
                picks[...], ext_own[LANES:, cut]
            )
        for copy in flying[step]:
            copy.start()

    def take_ghosts(step):
        for copy in flying[step]:
            copy.wait_recv()
        for b in range(ORB):
            high, low = halves(rbuf[step, b].T)
            ext_ghost[0:LANES, b * GHOST : (b + 1) * GHOST] = high
            ext_ghost[LANES:, b * GHOST : (b + 1) * GHOST] = low

    send_chain(1)
    multiply_own(2 * LANES)

    @pl.loop(0, (NEIGH - 1) // 2)
    def _(two):
        hot = onehot[:, pl.ds(pl.multiple_of(two * 2 * LANES + LANES, LANES), 2 * LANES)]
        both = dot(noise_ext[...], hot).astype(bf16)
        gathered[2 * two] = both[:, 0:LANES]
        gathered[2 * two + 1] = both[:, LANES:]

    take_ghosts(1)
    multiply_ghost(2 * LANES)
    chain[2] = 2.0 * (acc[0:LANES] + acc[LANES:]) - chain[0]
    res[...] += coef[2] * chain[2]

    send_chain(2)
    multiply_own(2 * LANES)
    take_ghosts(2)
    multiply_ghost(2 * LANES)
    res[...] += coef[3] * (2.0 * (acc[0:LANES] + acc[LANES:]) - chain[1])

    for a in range(ORB):
        w_out[a] = res[:, a * LANES : (a + 1) * LANES].T

    pairs[...] = jnp.zeros(pairs.shape, f32)

    @pl.loop(1, NEIGH)
    def _(m):
        columns = pl.ds(pl.multiple_of(m * LANES, LANES), LANES)
        for b in range(ORB):
            near = gathered[m - 1, b * LANES : (b + 1) * LANES].astype(f32)
            for a in range(ORB):
                term = res[:, a * LANES : (a + 1) * LANES] * near
                dens[a, b : b + 1] = jnp.sum(term, axis=0, keepdims=True)
        for c in range(3):
            total = deriv[c, m, 0].astype(f32) * dens[0]
            for a in range(1, ORB):
                total = total + deriv[c, m, a].astype(f32) * dens[a]
            pair = jnp.sum(total, axis=0, keepdims=True) * (1.0 / LANES)
            pairs[c : c + 1, columns] = pair
            pairs[c : c + 1, 0:LANES] -= pair

    high, low = halves(pairs[...])
    stacked = jnp.concatenate(
        [high, low, jnp.zeros((LANES - 16, NEIGH * LANES), bf16)], axis=0
    )
    spread = dot_t(onehot[...], stacked)
    fsend[...] = spread[LANES:EXT]

    back = []
    for at, (direction, first, rows) in enumerate(SEGMENTS):
        back.append(
            pltpu.make_async_remote_copy(
                src_ref=fsend.at[pl.ds(first, rows), :],
                dst_ref=frecv.at[pl.ds(first, rows), :],
                send_sem=send_sem.at[3, at],
                recv_sem=recv_sem.at[3, at],
                device_id=shifted(direction, 1),
                device_id_type=MESH,
            )
        )
    for copy in back:
        copy.start()
    own = spread[0:LANES].T[0:16]
    for copy in back:
        copy.wait_recv()
    high, low = halves(frecv[...].T[0:16])
    total = own + dot(high, picks[...]) + dot(low, picks[...])
    f_out[...] = total[0:3] + total[8:11]
    for copy in flying[0] + flying[1] + flying[2] + back:
        copy.wait_send()


def extended_slots(sizes, neighbours):
    atom_count = neighbours.shape[0]
    cell_count = CX * CY * CZ
    size_x, size_y, size_z = sizes
    ids = neighbours.T
    domain = ids // atom_count
    within = ids % atom_count
    basis = within // cell_count
    remain = within % cell_count
    parts = (
        (domain // (size_y * size_z), remain // (CY * CZ), "gx", CX, size_x),
        (domain // size_z % size_y, remain // CZ % CY, "gy", CY, size_y),
        (domain % size_z, remain % CZ, "gz", CZ, size_z),
    )
    signs = []
    inside = basis
    for dom, cell, axis, cells, size in parts:
        place = jnp.remainder((dom - lax.axis_index(axis)) * cells + cell + 1, cells * size)
        sign = jnp.where(place == 0, -1, jnp.where(place == cells + 1, 1, 0))
        signs.append(sign)
        inside = jnp.where(sign == 0, inside * cells + place - 1, inside)
    code = signs[0] * 9 + signs[1] * 3 + signs[2]
    first = jnp.zeros_like(code)
    for (dx, dy, dz), row, _ in SEGMENTS:
        first = jnp.where(code == dx * 9 + dy * 3 + dz, LANES + row, first)
    slots = first + inside
    return jnp.concatenate([slots, jnp.full((1, atom_count), -1, jnp.int32)], axis=0)


def shards(sizes, noise, ham, deriv, neighbours, coef):
    f32 = jnp.float32
    bf16 = jnp.bfloat16
    index = extended_slots(sizes, neighbours)
    picks = jnp.asarray(picking_matrix(), bf16)
    vmem = pl.BlockSpec(memory_space=pltpu.VMEM)
    smem = pl.BlockSpec(memory_space=pltpu.SMEM)
    return pl.pallas_call(
        functools.partial(kernel, sizes),
        out_shape=(
            jax.ShapeDtypeStruct((ORB, LANES, LANES), f32),
            jax.ShapeDtypeStruct((3, LANES), f32),
        ),
        in_specs=[vmem, vmem, vmem, vmem, smem, vmem],
        out_specs=(vmem, vmem),
        scratch_shapes=[
            pltpu.VMEM((ORB * LANES, WIDE), bf16),
            pltpu.VMEM((ORB * GHOST, WIDE), bf16),
            pltpu.VMEM((EXT, NEIGH * LANES), bf16),
            pltpu.VMEM((2 * LANES, ORB * LANES), bf16),
            pltpu.VMEM((2 * LANES, ORB * GHOST), bf16),
            pltpu.VMEM((WIDE, EXT), bf16),
            pltpu.VMEM((NEIGH - 1, WIDE, LANES), bf16),
            pltpu.VMEM((3, LANES, WIDE), f32),
            pltpu.VMEM((LANES, WIDE), f32),
            pltpu.VMEM((2 * LANES, WIDE), f32),
            pltpu.VMEM((3, ORB, GHOST, LANES), f32),
            pltpu.VMEM((3, ORB, GHOST, LANES), f32),
            pltpu.VMEM((GHOST, LANES), f32),
            pltpu.VMEM((GHOST, LANES), f32),
            pltpu.VMEM((8, NEIGH * LANES), f32),
            pltpu.VMEM((ORB, ORB, LANES), f32),
            pltpu.SemaphoreType.DMA((4, COPIES)),
            pltpu.SemaphoreType.DMA((4, COPIES)),
        ],
        compiler_params=pltpu.CompilerParams(
            collective_id=0, has_side_effects=True, vmem_limit_bytes=56 * 1024 * 1024
        ),
        name="fermi_forces",
    )(noise, ham, deriv, index, coef, picks)


def solution(mesh):
    sizes = tuple(mesh.shape[name] for name in ("gx", "gy", "gz"))
    in_specs = (
        P(None, ("gx", "gy", "gz"), None),
        P(None, None, None, ("gx", "gy", "gz")),
        P(None, None, None, None, ("gx", "gy", "gz")),
        P(("gx", "gy", "gz"), None),
        P(),
    )
    out_specs = (P(None, ("gx", "gy", "gz"), None), P(None, ("gx", "gy", "gz")))
    return jax.shard_map(
        functools.partial(shards, sizes),
        mesh=mesh,
        in_specs=in_specs,
        out_specs=out_specs,
        check_vma=False,
    )
```

profile of v0, /device:TPU:0, one launch (start us, length us, event | category | flops | bytes accessed | tf_op | source)
XLA Modules:
  0.0 113.4 jit_solution(513718784006131150)
XLA Ops:
  0.6 0.8 select_add_fusion
  1.4 0.6 concatenate.3.index
  2.0 1.9 %copy.8.ham = bf16[15,9,9,128]{3,2,1,0:T(8,128)(2,1)} copy(bf16[15,9,9,128]{3,0,2,1:T(8,128)(2,1)} %param.7) | data formatting | bytes 622080 | tf_op args[1]
  3.9 2.8 %copy.9.deriv = bf16[3,15,9,9,128]{4,3,2,1,0:T(8,128)(2,1)} copy(bf16[3,15,9,9,128]{4,1,3,2,0:T(8,128)(2,1)} %param.8) | data formatting | bytes 1866240 | tf_op args[2]
  6.7 103.6 %fermi_forces.1 = (f32[9,128,128]{2,1,0:T(8,128)}, f32[3,128]{1,0:T(4,128)}) custom-call(bf16[9,128,128]{2,1,0:T(8,128)(2,1)} %noise.1, bf16[15,9,9,128]{3,2,1,0:T(8,128)(2,1)} %copy.8.ham, bf16[3,15,9,9,128]{4,3,2,1,0:T(8,128)(2,1)} %copy.9.deriv, s32[16,128]{1,0:T(8,128)} %concatenate.3.index, f32[4]{0:T(128)} %coef.1, bf16[384,128]{1,0:T(8,128)(2,1)} %constant.248.clone.picks), custom_call_target="tpu_custom_call" | custom-call | tf_op jit(solution)/shard_map/fermi_forces/pallas_call | solution.py:335
  110.3 1.9 %copy.12 = f32[9,128,128]{2,1,0:T(8,128)} copy(f32[9,128,128]{2,1,0:T(8,128)} %get-tuple-element.4) | data formatting | bytes 1179648
  112.2 1.3 %copy.13 = f32[3,128]{1,0:T(4,128)} copy(f32[3,128]{1,0:T(4,128)} %get-tuple-element.5) | data formatting | bytes 3072
where the time goes:
time: 114 us; the launch traced here: 113 us
  Pallas kernels  104 us (91%)
  local copies, waits for them, and re-layouts  8.45 us (7%)
    pallas_call x1, Pallas kernels, shards(): pl.pallas_call(functools.partial(kernel, sizes), out_shape=(jax.ShapeDtyp...  104 us
    unnamed x4, local copies, waits for them, and re-layouts  7.85 us

commit v1 on v0

v1 whole, which is shorter than its diff:
```python
import functools

import jax
import jax.numpy as jnp
import numpy as np
from jax import lax
from jax.experimental import pallas as pl
from jax.experimental.pallas import tpu as pltpu
from jax.sharding import PartitionSpec as P

MESH = pl.DeviceIdType.MESH
CX = 4
CY = 4
CZ = 4
NEIGH = 15
ORB = 9
LANES = 128
HALF = 64
WIDE = ORB * LANES
FACE = 32
EDGE = 8
CORNER = 2
FACES = 6
EDGES = 12
CORNERS = 8
PICKED = FACES * FACE + EDGES * EDGE + CORNERS * CORNER
EXT = 512
FACE_ROWS = ORB * FACE
EDGE_ROWS = 80
CORNER_ROWS = 32
EDGE_AT = FACES * FACE_ROWS
CORNER_AT = EDGES * EDGE_ROWS
SMALL = CORNER_AT + CORNERS * CORNER_ROWS
GHOST = EDGE_AT + SMALL
SHARE = 384


def ghost_segments():
    kinds = ([], [], [])
    for dx in (-1, 0, 1):
        for dy in (-1, 0, 1):
            for dz in (-1, 0, 1):
                axes = abs(dx) + abs(dy) + abs(dz)
                if axes > 0:
                    kinds[axes - 1].append((dx, dy, dz))
    placed = []
    picked = 0
    sent = 0
    for group, atoms, rows in zip(
        kinds, (FACE, EDGE, CORNER), (FACE_ROWS, EDGE_ROWS, CORNER_ROWS)
    ):
        for direction in group:
            placed.append((direction, picked, sent, rows))
            picked += atoms
            sent += rows
    return placed


SEGMENTS = ghost_segments()
COPIES = len(SEGMENTS)


def picking_matrix():
    picks = np.zeros((PICKED, LANES), np.float32)
    for (dx, dy, dz), first, _, _ in SEGMENTS:
        row = first
        for basis in range(2):
            for x in range(CX) if dx == 0 else ((0,) if dx > 0 else (CX - 1,)):
                for y in range(CY) if dy == 0 else ((0,) if dy > 0 else (CY - 1,)):
                    for z in range(CZ) if dz == 0 else ((0,) if dz > 0 else (CZ - 1,)):
                        picks[row, ((basis * CX + x) * CY + y) * CZ + z] = 1.0
                        row += 1
    return picks


def segment_spans():
    spans = np.zeros((COPIES, 8, SHARE), np.float32)
    for at, (direction, first, _, _) in enumerate(SEGMENTS):
        axes = sum(abs(d) for d in direction)
        spans[at, :, first : first + (FACE, EDGE, CORNER)[axes - 1]] = 1.0
    return spans


def dot(a, b):
    return jnp.dot(a, b, preferred_element_type=jnp.float32)


def dot_t(a, b):
    return lax.dot_general(a, b, (((1,), (1,)), ((), ())), preferred_element_type=jnp.float32)


def halves(x):
    high = x.astype(jnp.bfloat16)
    return high, (x - high.astype(jnp.float32)).astype(jnp.bfloat16)


def kernel(
    sizes,
    noise,
    ham,
    deriv,
    index,
    coef,
    picks,
    spans,
    w_out,
    f_out,
    ht_own,
    ht_ghost,
    onehot,
    ext_own,
    ext_ghost,
    noise_ext,
    gathered,
    chain,
    res,
    acc,
    sbuf,
    rbuf,
    small,
    small_ham,
    fsend,
    frecv,
    pairs,
    dens,
    send_sem,
    recv_sem,
):
    f32 = jnp.float32
    bf16 = jnp.bfloat16
    here = [lax.axis_index(name) for name in ("gx", "gy", "gz")]

    def shifted(direction, sign):
        return tuple(
            lax.rem(me + size + sign * d, size) for me, size, d in zip(here, sizes, direction)
        )

    barrier = pltpu.get_barrier_semaphore()
    for direction, _, _, _ in SEGMENTS:
        pl.semaphore_signal(barrier, inc=1, device_id=shifted(direction, -1), device_id_type=MESH)

    def pack(step, rows_of):
        for b in range(ORB):
            rows = rows_of(b)
            for f in range(FACES):
                to = (f * ORB + b) * FACE
                sbuf[step, to : to + FACE] = rows[f * FACE : (f + 1) * FACE].astype(bf16)
            for e in range(EDGES):
                at = FACES * FACE + e * EDGE
                to = e * EDGE_ROWS + b * EDGE
                small[to : to + EDGE] = rows[at : at + EDGE]
            for c in range(CORNERS):
                at = FACES * FACE + EDGES * EDGE + c * CORNER
                to = CORNER_AT + c * CORNER_ROWS + b * CORNER
                small[to : to + CORNER] = rows[at : at + CORNER]
        sbuf[step, EDGE_AT:GHOST] = small[...].astype(bf16)

    def copies(step):
        made = []
        for at, (direction, _, first, rows) in enumerate(SEGMENTS):
            made.append(
                pltpu.make_async_remote_copy(
                    src_ref=sbuf.at[step, pl.ds(first, rows), :],
                    dst_ref=rbuf.at[step, pl.ds(first, rows), :],
                    send_sem=send_sem.at[step, at],
                    recv_sem=recv_sem.at[step, at],
                    device_id=shifted(direction, -1),
                    device_id_type=MESH,
                )
            )
        return made

    flying = [copies(step) for step in range(5)]

    small[...] = jnp.zeros(small.shape, f32)
    small_ham[...] = jnp.zeros(small_ham.shape, f32)
    pack(0, lambda b: dot(picks[...], noise[b]))
    pl.semaphore_wait(barrier, COPIES)
    for copy in flying[0]:
        copy.start()

    for b in range(ORB):
        turned = noise[b].astype(f32).T
        chain[0, :, b * LANES : (b + 1) * LANES] = turned
        ext_own[0:LANES, b * LANES : (b + 1) * LANES] = turned.astype(bf16)
        noise_ext[b * LANES : (b + 1) * LANES, 0:LANES] = turned.astype(bf16)

    @pl.loop(0, EXT // LANES)
    def _(part):
        first = pl.multiple_of(part * LANES, LANES)
        rows = lax.broadcasted_iota(jnp.int32, (LANES, LANES), 0) + first
        for m in range(NEIGH):
            same = rows == index[m : m + 1, :]
            onehot[pl.ds(first, LANES), m * LANES : (m + 1) * LANES] = jnp.where(
                same, 1.0, 0.0
            ).astype(bf16)

    @pl.loop(0, ORB)
    def _(a):
        columns = pl.ds(pl.multiple_of(a * LANES, LANES), LANES)
        for b in range(ORB):
            blocks = ham[a, b].astype(f32)
            rows = [
                jnp.broadcast_to(blocks[m : m + 1], (16, LANES)).astype(bf16)[None]
                for m in range(NEIGH)
            ]

            def block(first, count):
                total = None
                for m in range(NEIGH):
                    hot = onehot[first : first + count, m * LANES : (m + 1) * LANES]
                    term = hot.reshape(count // 16, 16, LANES) * rows[m]
                    total = term if total is None else total + term
                return total.reshape(count, LANES)

            ht_own[b * LANES : (b + 1) * LANES, columns] = block(0, LANES)
            for two in range(FACES // 2):
                made = block(LANES + two * 2 * FACE, 2 * FACE)
                for f in (2 * two, 2 * two + 1):
                    to = (f * ORB + b) * FACE
                    ht_ghost[to : to + FACE, columns] = made[(f % 2) * FACE : (f % 2 + 1) * FACE]
            made = block(LANES + FACES * FACE, EDGES * EDGE + CORNERS * CORNER).astype(f32)
            for e in range(EDGES):
                to = e * EDGE_ROWS + b * EDGE
                small_ham[to : to + EDGE] = made[e * EDGE : (e + 1) * EDGE]
            for c in range(CORNERS):
                at = EDGES * EDGE + c * CORNER
                to = CORNER_AT + c * CORNER_ROWS + b * CORNER
                small_ham[to : to + CORNER] = made[at : at + CORNER]
        ht_ghost[EDGE_AT:GHOST, columns] = small_ham[...].astype(bf16)

    def multiply(rows, ext, operator, first):
        @pl.loop(0, 3)
        def _(part):
            columns = pl.ds(pl.multiple_of(part * SHARE, SHARE), SHARE)
            product = dot(ext[rows], operator[:, columns])
            if first:
                acc[rows, columns] = product
            else:
                acc[rows, columns] += product

    def take(step, rows):
        for copy in flying[step]:
            copy.wait_recv()
        ext_ghost[rows] = rbuf[step].T

    vectors = (slice(0, HALF), slice(HALF, LANES))
    pieces = (slice(0, LANES), slice(LANES, 2 * LANES))

    def summed(half):
        base = half * LANES
        return acc[base : base + HALF] + acc[base + HALF : base + LANES]

    def send_half(order, half):
        high, low = halves(chain[order, vectors[half]])
        ext_own[half * LANES : half * LANES + HALF] = high
        ext_own[half * LANES + HALF : (half + 1) * LANES] = low
        step = 2 * order - 1 + half
        pack(
            step,
            lambda b: dot_t(picks[...], ext_own[pieces[half], b * LANES : (b + 1) * LANES]),
        )
        for copy in flying[step]:
            copy.start()

    multiply(pieces[0], ext_own, ht_own, True)
    take(0, pieces[0])
    multiply(pieces[0], ext_ghost, ht_ghost, False)
    chain[1] = acc[0:LANES]
    send_half(1, 0)
    send_half(1, 1)
    res[...] = coef[0] * chain[0] + coef[1] * chain[1]

    for b in range(ORB):
        parts = []
        for f in range(FACES):
            at = (f * ORB + b) * FACE
            parts.append(rbuf[0, at : at + FACE])
        noise_rows = jnp.concatenate(parts, axis=0)
        noise_ext[b * LANES : (b + 1) * LANES, LANES : LANES + FACES * FACE] = noise_rows.T
    small[...] = rbuf[0, EDGE_AT:GHOST].astype(f32)
    for b in range(ORB):
        parts = []
        for e in range(EDGES):
            at = e * EDGE_ROWS + b * EDGE
            parts.append(small[at : at + EDGE])
        for c in range(CORNERS):
            at = CORNER_AT + c * CORNER_ROWS + b * CORNER
            parts.append(small[at : at + CORNER])
        parts.append(jnp.zeros((EXT - LANES - PICKED, LANES), f32))
        noise_rows = jnp.concatenate(parts, axis=0).astype(bf16)
        noise_ext[b * LANES : (b + 1) * LANES, LANES + FACES * FACE : EXT] = noise_rows.T

    multiply(slice(0, 2 * LANES), ext_own, ht_own, True)

    @pl.loop(0, (NEIGH - 1) // 2)
    def _(two):
        hot = onehot[:, pl.ds(pl.multiple_of(two * 2 * LANES + LANES, LANES), 2 * LANES)]
        both = dot(noise_ext[...], hot).astype(bf16)
        gathered[2 * two] = both[:, 0:LANES]
        gathered[2 * two + 1] = both[:, LANES:]

    for half in range(2):
        take(1 + half, pieces[half])
        multiply(pieces[half], ext_ghost, ht_ghost, False)
        chain[2, vectors[half]] = 2.0 * summed(half) - chain[0, vectors[half]]
        send_half(2, half)
        multiply(pieces[half], ext_own, ht_own, True)
    res[...] += coef[2] * chain[2]

    dens[:, 0:1] = jnp.zeros((ORB * ORB, 1, LANES), f32)

    for half in range(2):
        take(3 + half, pieces[half])
        multiply(pieces[half], ext_ghost, ht_ghost, False)
        res[vectors[half]] += coef[3] * (2.0 * summed(half) - chain[1, vectors[half]])

        @pl.loop(1, NEIGH)
        def _(m):
            for b in range(ORB):
                base = b * LANES + half * HALF
                near = gathered[m - 1, base : base + HALF].astype(f32)
                for a in range(ORB):
                    term = res[vectors[half], a * LANES : (a + 1) * LANES] * near
                    row = jnp.sum(term, axis=0, keepdims=True)
                    if half == 0:
                        dens[a * ORB + b, pl.ds(m, 1)] = row
                    else:
                        dens[a * ORB + b, pl.ds(m, 1)] += row

    pairs[...] = jnp.zeros(pairs.shape, f32)
    for c in range(3):
        def add(ab, total):
            return total + deriv[c, ab].astype(f32) * dens[ab, 0:NEIGH]

        total = lax.fori_loop(0, ORB * ORB, add, jnp.zeros((NEIGH, LANES), f32), unroll=9)
        pair = total * (1.0 / LANES)
        pairs[c : c + 1, 0:LANES] = -jnp.sum(pair, axis=0, keepdims=True)
        for m in range(1, NEIGH):
            pairs[c : c + 1, m * LANES : (m + 1) * LANES] = pair[m : m + 1]
    high, low = halves(pairs[...])
    spread = dot_t(jnp.concatenate([high, low], axis=0), onehot[...])
    spread = spread[0:8] + spread[8:16]
    high, low = halves(spread[:, LANES:EXT])
    mask = spans[...]
    shape = (COPIES * 8, SHARE)
    high = (high.astype(f32)[None] * mask).reshape(shape).astype(bf16)
    low = (low.astype(f32)[None] * mask).reshape(shape).astype(bf16)
    tiles = dot(high[:, 0:PICKED], picks[...]) + dot(low[:, 0:PICKED], picks[...])
    fsend[...] = tiles.reshape(COPIES, 8, LANES)

    back = []
    for at, (direction, _, _, _) in enumerate(SEGMENTS):
        back.append(
            pltpu.make_async_remote_copy(
                src_ref=fsend.at[at],
                dst_ref=frecv.at[at],
                send_sem=send_sem.at[5, at],
                recv_sem=recv_sem.at[5, at],
                device_id=shifted(direction, 1),
                device_id_type=MESH,
            )
        )
    for copy in back:
        copy.start()
    for a in range(ORB):
        w_out[a] = res[:, a * LANES : (a + 1) * LANES].T
    for copy in back:
        copy.wait_recv()
    total = spread[:, 0:LANES]
    for at in range(COPIES):
        total = total + frecv[at]
    f_out[...] = total[0:3]
    for group in flying:
        for copy in group:
            copy.wait_send()
    for copy in back:
        copy.wait_send()


def extended_slots(sizes, neighbours):
    atom_count = neighbours.shape[0]
    cell_count = CX * CY * CZ
    size_x, size_y, size_z = sizes
    ids = neighbours.T
    domain = ids // atom_count
    within = ids % atom_count
    basis = within // cell_count
    remain = within % cell_count
    parts = (
        (domain // (size_y * size_z), remain // (CY * CZ), "gx", CX, size_x),
        (domain // size_z % size_y, remain // CZ % CY, "gy", CY, size_y),
        (domain % size_z, remain % CZ, "gz", CZ, size_z),
    )
    signs = []
    inside = basis
    for dom, cell, axis, cells, size in parts:
        place = jnp.remainder((dom - lax.axis_index(axis)) * cells + cell + 1, cells * size)
        sign = jnp.where(place == 0, -1, jnp.where(place == cells + 1, 1, 0))
        signs.append(sign)
        inside = jnp.where(sign == 0, inside * cells + place - 1, inside)
    code = signs[0] * 9 + signs[1] * 3 + signs[2]
    first = jnp.zeros_like(code)
    for (dx, dy, dz), row, _, _ in SEGMENTS:
        first = jnp.where(code == dx * 9 + dy * 3 + dz, LANES + row, first)
    return first + inside


def shards(sizes, noise, ham, deriv, neighbours, coef):
    f32 = jnp.float32
    bf16 = jnp.bfloat16
    index = extended_slots(sizes, neighbours)
    ham = ham.transpose(1, 2, 0, 3)
    deriv = deriv.transpose(0, 2, 3, 1, 4).reshape(3, ORB * ORB, NEIGH, LANES)
    picks = jnp.asarray(picking_matrix(), bf16)
    spans = jnp.asarray(segment_spans(), f32)
    vmem = pl.BlockSpec(memory_space=pltpu.VMEM)
    smem = pl.BlockSpec(memory_space=pltpu.SMEM)
    return pl.pallas_call(
        functools.partial(kernel, sizes),
        out_shape=(
            jax.ShapeDtypeStruct((ORB, LANES, LANES), f32),
            jax.ShapeDtypeStruct((3, LANES), f32),
        ),
        in_specs=[vmem, vmem, vmem, vmem, smem, vmem, vmem],
        out_specs=(vmem, vmem),
        scratch_shapes=[
            pltpu.VMEM((WIDE, WIDE), bf16),
            pltpu.VMEM((GHOST, WIDE), bf16),
            pltpu.VMEM((EXT, NEIGH * LANES), bf16),
            pltpu.VMEM((2 * LANES, WIDE), bf16),
            pltpu.VMEM((2 * LANES, GHOST), bf16),
            pltpu.VMEM((WIDE, EXT), bf16),
            pltpu.VMEM((NEIGH - 1, WIDE, LANES), bf16),
            pltpu.VMEM((3, LANES, WIDE), f32),
            pltpu.VMEM((LANES, WIDE), f32),
            pltpu.VMEM((2 * LANES, WIDE), f32),
            pltpu.VMEM((5, GHOST, LANES), bf16),
            pltpu.VMEM((5, GHOST, LANES), bf16),
            pltpu.VMEM((SMALL, LANES), f32),
            pltpu.VMEM((SMALL, LANES), f32),
            pltpu.VMEM((COPIES, 8, LANES), f32),
            pltpu.VMEM((COPIES, 8, LANES), f32),
            pltpu.VMEM((8, NEIGH * LANES), f32),
            pltpu.VMEM((ORB * ORB, 16, LANES), f32),
            pltpu.SemaphoreType.DMA((6, COPIES)),
            pltpu.SemaphoreType.DMA((6, COPIES)),
        ],
        compiler_params=pltpu.CompilerParams(
            collective_id=0, has_side_effects=True, vmem_limit_bytes=56 * 1024 * 1024
        ),
        name="fermi_forces",
    )(noise, ham, deriv, index, coef, picks, spans)


def solution(mesh):
    sizes = tuple(mesh.shape[name] for name in ("gx", "gy", "gz"))
    in_specs = (
        P(None, ("gx", "gy", "gz"), None),
        P(None, None, None, ("gx", "gy", "gz")),
        P(None, None, None, None, ("gx", "gy", "gz")),
        P(("gx", "gy", "gz"), None),
        P(),
    )
    out_specs = (P(None, ("gx", "gy", "gz"), None), P(None, ("gx", "gy", "gz")))
    return jax.shard_map(
        functools.partial(shards, sizes),
        mesh=mesh,
        in_specs=in_specs,
        out_specs=out_specs,
        check_vma=False,
    )
```

time: 114 us -> 87.3 us (0.77)
  Pallas kernels: 104 us -> 82.5 us
  local copies, waits for them, and re-layouts: 8.45 us -> 3.19 us
    pallas_call x1, Pallas kernels: 104 us -> 82.5 us  [shards(): pl.pallas_call(functools.partial(kernel, sizes), out_shape=(jax.ShapeDtyp...]
    unnamed x4 -> x6, local copies, waits for them, and re-layouts: 7.85 us -> 3.19 us
where the time goes in v1:
time: 87.3 us; the launch traced here: 87 us
  Pallas kernels  82.5 us (95%)
  local copies, waits for them, and re-layouts  3.19 us (4%)
    pallas_call x1, Pallas kernels, shards(): pl.pallas_call(functools.partial(kernel, sizes), out_shape=(jax.ShapeDtyp...  82.5 us
    unnamed x6, local copies, waits for them, and re-layouts  3.19 us

profile of v1, /device:TPU:0, one launch (start us, length us, event | category | flops | bytes accessed | tf_op | source)
XLA Modules:
  0.0 87.0 jit_solution(13269274760508576733)
XLA Ops:
  0.6 0.0 copy-start
  0.6 0.7 copy-done
  1.3 0.7 select_add_fusion.index
  2.0 82.5 %fermi_forces.1 = (f32[9,128,128]{2,1,0:T(8,128)}, f32[3,128]{1,0:T(4,128)}) custom-call(bf16[9,128,128]{2,1,0:T(8,128)(2,1)} %noise.1, bf16[9,9,15,128]{3,2,1,0:T(8,128)(2,1)} %bitcast.23, bf16[3,81,15,128]{3,2,1,0:T(8,128)(2,1)} %bitcast.22, s32[15,128]{1,0:T(8,128)} %select_add_fusion.index, f32[4]{0:T(128)} %coef.1, ...), custom_call_target="tpu_custom_call" | custom-call | tf_op jit(solution)/shard_map/fermi_forces/pallas_call | solution.py:419
  84.5 0.0 copy-start.1
  84.5 1.9 %copy.11 = f32[9,128,128]{2,1,0:T(8,128)} copy(f32[9,128,128]{2,1,0:T(8,128)} %get-tuple-element.4) | data formatting | bytes 1179648
  86.5 0.0 copy-done.1
  86.5 0.6 copy.12
Async XLA Ops:
  0.6 0.7 copy-start
  84.5 1.9 %copy-start.1 = (f32[3,128]{1,0:T(4,128)S(1)}, f32[3,128]{1,0:T(4,128)}, u32[]{:S(2)}) copy-start(f32[3,128]{1,0:T(4,128)} %get-tuple-element.5) | copy-start | bytes 4612

commit v2 on v1

--- a/solution.py
+++ b/solution.py
@@ -21,63 +21,81 @@
 EDGE = 8
 CORNER = 2
 FACES = 6
-EDGES = 12
-CORNERS = 8
-PICKED = FACES * FACE + EDGES * EDGE + CORNERS * CORNER
+EDGES = 4
+DIRECT = FACES * FACE + EDGES * EDGE
+RELAY = 4 * EDGE + 4 * CORNER
+PICKED = DIRECT + 2 * RELAY
 EXT = 512
 FACE_ROWS = ORB * FACE
 EDGE_ROWS = 80
-CORNER_ROWS = 32
+RELAY_ROWS = 368
 EDGE_AT = FACES * FACE_ROWS
-CORNER_AT = EDGES * EDGE_ROWS
-SMALL = CORNER_AT + CORNERS * CORNER_ROWS
-GHOST = EDGE_AT + SMALL
+RELAY_AT = EDGE_AT + EDGES * EDGE_ROWS
+SENT = RELAY_AT + 2 * RELAY_ROWS
+GHOST = SENT + 32
+SMALL = GHOST - EDGE_AT
 SHARE = 384
+HELD = ((-1, 0, 0), (1, 0, 0), (0, 0, -1), (0, 0, 1), (-1, 0, -1), (-1, 0, 1), (1, 0, -1), (1, 0, 1))
 
 
 def ghost_segments():
-    kinds = ([], [], [])
-    for dx in (-1, 0, 1):
-        for dy in (-1, 0, 1):
-            for dz in (-1, 0, 1):
-                axes = abs(dx) + abs(dy) + abs(dz)
-                if axes > 0:
-                    kinds[axes - 1].append((dx, dy, dz))
+    order = HELD[0:4] + ((0, -1, 0), (0, 1, 0)) + HELD[4:8]
+    for dy in (-1, 1):
+        order = order + tuple((dx, dy, dz) for dx, _, dz in HELD)
     placed = []
-    picked = 0
-    sent = 0
-    for group, atoms, rows in zip(
-        kinds, (FACE, EDGE, CORNER), (FACE_ROWS, EDGE_ROWS, CORNER_ROWS)
-    ):
-        for direction in group:
-            placed.append((direction, picked, sent, rows))
-            picked += atoms
-            sent += rows
+    first = 0
+    for direction in order:
+        placed.append((direction, first, atoms_in(direction)))
+        first += atoms_in(direction)
     return placed
+
+
+def atoms_in(direction):
+    return (FACE, EDGE, CORNER)[sum(abs(d) for d in direction) - 1]
 
 
 SEGMENTS = ghost_segments()
 COPIES = len(SEGMENTS)
 
 
+def cells_of(d, cells):
+    return range(cells) if d == 0 else ((0,) if d > 0 else (cells - 1,))
+
+
 def picking_matrix():
     picks = np.zeros((PICKED, LANES), np.float32)
-    for (dx, dy, dz), first, _, _ in SEGMENTS:
-        row = first
+    row = 0
+    for (dx, dy, dz), _, _ in SEGMENTS:
         for basis in range(2):
-            for x in range(CX) if dx == 0 else ((0,) if dx > 0 else (CX - 1,)):
-                for y in range(CY) if dy == 0 else ((0,) if dy > 0 else (CY - 1,)):
-                    for z in range(CZ) if dz == 0 else ((0,) if dz > 0 else (CZ - 1,)):
+            for x in cells_of(dx, CX):
+                for y in cells_of(dy, CY):
+                    for z in cells_of(dz, CZ):
                         picks[row, ((basis * CX + x) * CY + y) * CZ + z] = 1.0
                         row += 1
     return picks
 
 
+def relaying_matrix():
+    picks = np.zeros((2 * RELAY, 4 * FACE + 4 * EDGE), np.float32)
+    row = 0
+    for dy in (-1, 1):
+        held = 0
+        for dx, _, dz in HELD:
+            for basis in range(2):
+                for x in cells_of(dx, CX):
+                    for y in range(CY):
+                        for z in cells_of(dz, CZ):
+                            if y in cells_of(dy, CY):
+                                picks[row, held] = 1.0
+                                row += 1
+                            held += 1
+    return picks
+
+
 def segment_spans():
     spans = np.zeros((COPIES, 8, SHARE), np.float32)
-    for at, (direction, first, _, _) in enumerate(SEGMENTS):
-        axes = sum(abs(d) for d in direction)
-        spans[at, :, first : first + (FACE, EDGE, CORNER)[axes - 1]] = 1.0
+    for at, (_, first, count) in enumerate(SEGMENTS):
+        spans[at, :, first : first + count] = 1.0
     return spans
 
 
@@ -102,6 +120,7 @@
     index,
     coef,
     picks,
+    relays,
     spans,
     w_out,
     f_out,
@@ -119,6 +138,9 @@
     rbuf,
     small,
     small_ham,
+    small_relay,
+    near_slot,
+    far_slot,
     fsend,
     frecv,
     pairs,
@@ -136,7 +158,7 @@
         )
 
     barrier = pltpu.get_barrier_semaphore()
-    for direction, _, _, _ in SEGMENTS:
+    for direction, _, _ in SEGMENTS:
         pl.semaphore_signal(barrier, inc=1, device_id=shifted(direction, -1), device_id_type=MESH)
 
     def pack(step, rows_of):
@@ -149,32 +171,66 @@
                 at = FACES * FACE + e * EDGE
                 to = e * EDGE_ROWS + b * EDGE
                 small[to : to + EDGE] = rows[at : at + EDGE]
-            for c in range(CORNERS):
-                at = FACES * FACE + EDGES * EDGE + c * CORNER
-                to = CORNER_AT + c * CORNER_ROWS + b * CORNER
-                small[to : to + CORNER] = rows[at : at + CORNER]
-        sbuf[step, EDGE_AT:GHOST] = small[...].astype(bf16)
+        sbuf[step, EDGE_AT:RELAY_AT] = small[0 : EDGES * EDGE_ROWS].astype(bf16)
+
+    def copy_rows(step, at, first, rows, direction):
+        return pltpu.make_async_remote_copy(
+            src_ref=sbuf.at[step, pl.ds(first, rows), :],
+            dst_ref=rbuf.at[step, pl.ds(first, rows), :],
+            send_sem=send_sem.at[step, at],
+            recv_sem=recv_sem.at[step, at],
+            device_id=shifted(direction, -1),
+            device_id_type=MESH,
+        )
 
     def copies(step):
         made = []
-        for at, (direction, _, first, rows) in enumerate(SEGMENTS):
-            made.append(
-                pltpu.make_async_remote_copy(
-                    src_ref=sbuf.at[step, pl.ds(first, rows), :],
-                    dst_ref=rbuf.at[step, pl.ds(first, rows), :],
-                    send_sem=send_sem.at[step, at],
-                    recv_sem=recv_sem.at[step, at],
-                    device_id=shifted(direction, -1),
-                    device_id_type=MESH,
-                )
-            )
+        for at, (direction, _, _) in enumerate(SEGMENTS[0 : FACES + EDGES]):
+            if at < FACES:
+                made.append(copy_rows(step, at, at * FACE_ROWS, FACE_ROWS, direction))
+            else:
+                first = EDGE_AT + (at - FACES) * EDGE_ROWS
+                made.append(copy_rows(step, at, first, EDGE_ROWS, direction))
         return made
 
+    def relay_copies(step):
+        made = []
+        for at, dy in enumerate((-1, 1)):
+            first = RELAY_AT + at * RELAY_ROWS
+            made.append(copy_rows(step, FACES + EDGES + at, first, RELAY_ROWS, (0, dy, 0)))
+        return made
+
     flying = [copies(step) for step in range(5)]
+    relayed = [relay_copies(step) for step in range(5)]
+
+    def pass_on(step):
+        for copy in flying[step]:
+            copy.wait_recv()
+        edges = rbuf[step, EDGE_AT:RELAY_AT].astype(f32)
+        for b in range(ORB):
+            parts = []
+            for f in range(4):
+                at = (f * ORB + b) * FACE
+                parts.append(rbuf[step, at : at + FACE])
+            lines = []
+            for e in range(EDGES):
+                at = e * EDGE_ROWS + b * EDGE
+                lines.append(edges[at : at + EDGE])
+            parts.append(jnp.concatenate(lines, axis=0).astype(bf16))
+            rows = dot(relays[...], jnp.concatenate(parts, axis=0))
+            for side in range(2):
+                to = side * RELAY_ROWS + b * RELAY
+                small_relay[to : to + RELAY] = rows[side * RELAY : (side + 1) * RELAY]
+        sbuf[step, RELAY_AT:SENT] = small_relay[...].astype(bf16)
+        for copy in relayed[step]:
+            copy.start()
 
     small[...] = jnp.zeros(small.shape, f32)
     small_ham[...] = jnp.zeros(small_ham.shape, f32)
-    pack(0, lambda b: dot(picks[...], noise[b]))
+    small_relay[...] = jnp.zeros(small_relay.shape, f32)
+    for step in range(5):
+        rbuf[step, SENT:GHOST] = jnp.zeros((GHOST - SENT, LANES), bf16)
+    pack(0, lambda b: dot(picks[0:DIRECT], noise[b]))
     pl.semaphore_wait(barrier, COPIES)
     for copy in flying[0]:
         copy.start()
@@ -195,54 +251,78 @@
                 same, 1.0, 0.0
             ).astype(bf16)
 
-    @pl.loop(0, ORB)
-    def _(a):
+    @pl.loop(0, (LANES + PICKED) // 8)
+    def _(part):
+        first = pl.multiple_of(part * 8, 8)
+        rows = lax.broadcasted_iota(jnp.int32, (8, LANES), 0) + first
+        for found, low in ((near_slot, 1), (far_slot, 8)):
+            which = jnp.full((8, LANES), 7, jnp.int32)
+            for at in range(7):
+                which = jnp.where(rows == index[low + at : low + at + 1, :], at, which)
+            found[pl.ds(first, 8)] = which
+
+    def fill_columns(a):
         columns = pl.ds(pl.multiple_of(a * LANES, LANES), LANES)
+        last = lax.broadcasted_iota(jnp.int32, (8, LANES), 0) == 7
         for b in range(ORB):
             blocks = ham[a, b].astype(f32)
-            rows = [
-                jnp.broadcast_to(blocks[m : m + 1], (16, LANES)).astype(bf16)[None]
-                for m in range(NEIGH)
-            ]
+            itself = blocks[0:1]
+            tables = []
+            for low in (1, 8):
+                rows = jnp.concatenate([blocks[low : low + 7], blocks[0:1]], axis=0)
+                tables.append(jnp.where(last, 0.0, rows))
 
             def block(first, count):
-                total = None
-                for m in range(NEIGH):
-                    hot = onehot[first : first + count, m * LANES : (m + 1) * LANES]
-                    term = hot.reshape(count // 16, 16, LANES) * rows[m]
-                    total = term if total is None else total + term
-                return total.reshape(count, LANES)
-
-            ht_own[b * LANES : (b + 1) * LANES, columns] = block(0, LANES)
-            for two in range(FACES // 2):
-                made = block(LANES + two * 2 * FACE, 2 * FACE)
-                for f in (2 * two, 2 * two + 1):
-                    to = (f * ORB + b) * FACE
-                    ht_ghost[to : to + FACE, columns] = made[(f % 2) * FACE : (f % 2 + 1) * FACE]
-            made = block(LANES + FACES * FACE, EDGES * EDGE + CORNERS * CORNER).astype(f32)
+                made = []
+                for at in range(first, first + count, 8):
+                    made.append(
+                        jnp.take_along_axis(tables[0], near_slot[at : at + 8], axis=0)
+                        + jnp.take_along_axis(tables[1], far_slot[at : at + 8], axis=0)
+                    )
+                return jnp.concatenate(made, axis=0)
+
+            own = block(0, LANES)
+            shape = (LANES, LANES)
+            same = lax.broadcasted_iota(jnp.int32, shape, 0) == lax.broadcasted_iota(
+                jnp.int32, shape, 1
+            )
+            own = jnp.where(same, itself, own)
+            ht_own[b * LANES : (b + 1) * LANES, columns] = own.astype(bf16)
+            for f in range(FACES):
+                to = (f * ORB + b) * FACE
+                made = block(LANES + f * FACE, FACE)
+                ht_ghost[to : to + FACE, columns] = made.astype(bf16)
             for e in range(EDGES):
                 to = e * EDGE_ROWS + b * EDGE
-                small_ham[to : to + EDGE] = made[e * EDGE : (e + 1) * EDGE]
-            for c in range(CORNERS):
-                at = EDGES * EDGE + c * CORNER
-                to = CORNER_AT + c * CORNER_ROWS + b * CORNER
-                small_ham[to : to + CORNER] = made[at : at + CORNER]
+                small_ham[to : to + EDGE] = block(LANES + FACES * FACE + e * EDGE, EDGE)
+            for side in range(2):
+                to = RELAY_AT - EDGE_AT + side * RELAY_ROWS + b * RELAY
+                small_ham[to : to + RELAY] = block(LANES + DIRECT + side * RELAY, RELAY)
         ht_ghost[EDGE_AT:GHOST, columns] = small_ham[...].astype(bf16)
 
-    def multiply(rows, ext, operator, first):
+    pl.loop(0, 5)(fill_columns)
+    pass_on(0)
+    pl.loop(5, ORB)(fill_columns)
+
+    def multiply(rows, ext, operator, first, span=slice(None)):
         @pl.loop(0, 3)
         def _(part):
             columns = pl.ds(pl.multiple_of(part * SHARE, SHARE), SHARE)
-            product = dot(ext[rows], operator[:, columns])
+            product = dot(ext[rows, span], operator[span, columns])
             if first:
                 acc[rows, columns] = product
             else:
                 acc[rows, columns] += product
 
-    def take(step, rows):
-        for copy in flying[step]:
+    def multiply_ghosts(step, rows):
+        if step > 0:
+            pass_on(step)
+        ext_ghost[rows, 0:RELAY_AT] = rbuf[step, 0:RELAY_AT].T
+        multiply(rows, ext_ghost, ht_ghost, False, slice(0, RELAY_AT))
+        for copy in relayed[step]:
             copy.wait_recv()
-        ext_ghost[rows] = rbuf[step].T
+        ext_ghost[rows, RELAY_AT:GHOST] = rbuf[step, RELAY_AT:GHOST].T
+        multiply(rows, ext_ghost, ht_ghost, False, slice(RELAY_AT, GHOST))
 
     vectors = (slice(0, HALF), slice(HALF, LANES))
     pieces = (slice(0, LANES), slice(LANES, 2 * LANES))
@@ -258,14 +338,13 @@
         step = 2 * order - 1 + half
         pack(
             step,
-            lambda b: dot_t(picks[...], ext_own[pieces[half], b * LANES : (b + 1) * LANES]),
+            lambda b: dot_t(picks[0:DIRECT], ext_own[pieces[half], b * LANES : (b + 1) * LANES]),
         )
         for copy in flying[step]:
             copy.start()
 
     multiply(pieces[0], ext_own, ht_own, True)
-    take(0, pieces[0])
-    multiply(pieces[0], ext_ghost, ht_ghost, False)
+    multiply_ghosts(0, pieces[0])
     chain[1] = acc[0:LANES]
     send_half(1, 0)
     send_half(1, 1)
@@ -278,15 +357,15 @@
             parts.append(rbuf[0, at : at + FACE])
         noise_rows = jnp.concatenate(parts, axis=0)
         noise_ext[b * LANES : (b + 1) * LANES, LANES : LANES + FACES * FACE] = noise_rows.T
-    small[...] = rbuf[0, EDGE_AT:GHOST].astype(f32)
+    small_ghost = rbuf[0, EDGE_AT:GHOST].astype(f32)
     for b in range(ORB):
         parts = []
         for e in range(EDGES):
             at = e * EDGE_ROWS + b * EDGE
-            parts.append(small[at : at + EDGE])
-        for c in range(CORNERS):
-            at = CORNER_AT + c * CORNER_ROWS + b * CORNER
-            parts.append(small[at : at + CORNER])
+            parts.append(small_ghost[at : at + EDGE])
+        for side in range(2):
+            at = RELAY_AT - EDGE_AT + side * RELAY_ROWS + b * RELAY
+            parts.append(small_ghost[at : at + RELAY])
         parts.append(jnp.zeros((EXT - LANES - PICKED, LANES), f32))
         noise_rows = jnp.concatenate(parts, axis=0).astype(bf16)
         noise_ext[b * LANES : (b + 1) * LANES, LANES + FACES * FACE : EXT] = noise_rows.T
@@ -301,8 +380,7 @@
         gathered[2 * two + 1] = both[:, LANES:]
 
     for half in range(2):
-        take(1 + half, pieces[half])
-        multiply(pieces[half], ext_ghost, ht_ghost, False)
+        multiply_ghosts(1 + half, pieces[half])
         chain[2, vectors[half]] = 2.0 * summed(half) - chain[0, vectors[half]]
         send_half(2, half)
         multiply(pieces[half], ext_own, ht_own, True)
@@ -311,8 +389,7 @@
     dens[:, 0:1] = jnp.zeros((ORB * ORB, 1, LANES), f32)
 
     for half in range(2):
-        take(3 + half, pieces[half])
-        multiply(pieces[half], ext_ghost, ht_ghost, False)
+        multiply_ghosts(3 + half, pieces[half])
         res[vectors[half]] += coef[3] * (2.0 * summed(half) - chain[1, vectors[half]])
 
         @pl.loop(1, NEIGH)
@@ -350,7 +427,7 @@
     fsend[...] = tiles.reshape(COPIES, 8, LANES)
 
     back = []
-    for at, (direction, _, _, _) in enumerate(SEGMENTS):
+    for at, (direction, _, _) in enumerate(SEGMENTS):
         back.append(
             pltpu.make_async_remote_copy(
                 src_ref=fsend.at[at],
@@ -371,7 +448,7 @@
     for at in range(COPIES):
         total = total + frecv[at]
     f_out[...] = total[0:3]
-    for group in flying:
+    for group in flying + relayed:
         for copy in group:
             copy.wait_send()
     for copy in back:
@@ -401,7 +478,7 @@
         inside = jnp.where(sign == 0, inside * cells + place - 1, inside)
     code = signs[0] * 9 + signs[1] * 3 + signs[2]
     first = jnp.zeros_like(code)
-    for (dx, dy, dz), row, _, _ in SEGMENTS:
+    for (dx, dy, dz), row, _ in SEGMENTS:
         first = jnp.where(code == dx * 9 + dy * 3 + dz, LANES + row, first)
     return first + inside
 
@@ -413,6 +490,7 @@
     ham = ham.transpose(1, 2, 0, 3)
     deriv = deriv.transpose(0, 2, 3, 1, 4).reshape(3, ORB * ORB, NEIGH, LANES)
     picks = jnp.asarray(picking_matrix(), bf16)
+    relays = jnp.asarray(relaying_matrix(), bf16)
     spans = jnp.asarray(segment_spans(), f32)
     vmem = pl.BlockSpec(memory_space=pltpu.VMEM)
     smem = pl.BlockSpec(memory_space=pltpu.SMEM)
@@ -422,7 +500,7 @@
             jax.ShapeDtypeStruct((ORB, LANES, LANES), f32),
             jax.ShapeDtypeStruct((3, LANES), f32),
         ),
-        in_specs=[vmem, vmem, vmem, vmem, smem, vmem, vmem],
+        in_specs=[vmem, vmem, vmem, vmem, smem, vmem, vmem, vmem],
         out_specs=(vmem, vmem),
         scratch_shapes=[
             pltpu.VMEM((WIDE, WIDE), bf16),
@@ -435,10 +513,13 @@
             pltpu.VMEM((3, LANES, WIDE), f32),
             pltpu.VMEM((LANES, WIDE), f32),
             pltpu.VMEM((2 * LANES, WIDE), f32),
+            pltpu.VMEM((5, SENT, LANES), bf16),
             pltpu.VMEM((5, GHOST, LANES), bf16),
-            pltpu.VMEM((5, GHOST, LANES), bf16),
+            pltpu.VMEM((EDGES * EDGE_ROWS, LANES), f32),
             pltpu.VMEM((SMALL, LANES), f32),
-            pltpu.VMEM((SMALL, LANES), f32),
+            pltpu.VMEM((2 * RELAY_ROWS, LANES), f32),
+            pltpu.VMEM((LANES + PICKED, LANES), jnp.int32),
+            pltpu.VMEM((LANES + PICKED, LANES), jnp.int32),
             pltpu.VMEM((COPIES, 8, LANES), f32),
             pltpu.VMEM((COPIES, 8, LANES), f32),
             pltpu.VMEM((8, NEIGH * LANES), f32),
@@ -450,7 +531,7 @@
             collective_id=0, has_side_effects=True, vmem_limit_bytes=56 * 1024 * 1024
         ),
         name="fermi_forces",
-    )(noise, ham, deriv, index, coef, picks, spans)
+    )(noise, ham, deriv, index, coef, picks, relays, spans)
 
 
 def solution(mesh):

time: 87.3 us -> 76.5 us (0.88)
  Pallas kernels: 82.5 us -> 71.8 us
    pallas_call x1, Pallas kernels: 82.5 us -> 71.8 us  [shards(): pl.pallas_call(functools.partial(kernel, sizes), out_shape=(jax.ShapeDtyp...]
where the time goes in v2:
time: 76.5 us; the launch traced here: 76.3 us
  Pallas kernels  71.8 us (94%)
  local copies, waits for them, and re-layouts  3.19 us (4%)
    pallas_call x1, Pallas kernels, shards(): pl.pallas_call(functools.partial(kernel, sizes), out_shape=(jax.ShapeDtyp...  71.8 us
    unnamed x6, local copies, waits for them, and re-layouts  3.19 us

profile of v2, /device:TPU:0, one launch (start us, length us, event | category | flops | bytes accessed | tf_op | source)
XLA Modules:
  0.0 76.3 jit_solution(8751744250431171865)
XLA Ops:
  0.6 0.0 copy-start
  0.6 0.7 copy-done
  1.3 0.7 select_add_fusion.index
  2.0 71.8 %fermi_forces.1 = (f32[9,128,128]{2,1,0:T(8,128)}, f32[3,128]{1,0:T(4,128)}) custom-call(bf16[9,128,128]{2,1,0:T(8,128)(2,1)} %noise.1, bf16[9,9,15,128]{3,2,1,0:T(8,128)(2,1)} %bitcast.23, bf16[3,81,15,128]{3,2,1,0:T(8,128)(2,1)} %bitcast.22, s32[15,128]{1,0:T(8,128)} %select_add_fusion.index, f32[4]{0:T(128)} %coef.1, ...), custom_call_target="tpu_custom_call" | custom-call | tf_op jit(solution)/shard_map/fermi_forces/pallas_call | solution.py:497
  73.8 0.0 copy-start.1
  73.8 1.9 %copy.12 = f32[9,128,128]{2,1,0:T(8,128)} copy(f32[9,128,128]{2,1,0:T(8,128)} %get-tuple-element.4) | data formatting | bytes 1179648
  75.7 0.0 copy-done.1
  75.7 0.6 copy.13
Async XLA Ops:
  0.6 0.7 copy-start
  73.8 1.9 %copy-start.1 = (f32[3,128]{1,0:T(4,128)S(1)}, f32[3,128]{1,0:T(4,128)}, u32[]{:S(2)}) copy-start(f32[3,128]{1,0:T(4,128)} %get-tuple-element.5) | copy-start | bytes 4612

commit v3 on v2

--- a/solution.py
+++ b/solution.py
@@ -33,8 +33,9 @@
 RELAY_AT = EDGE_AT + EDGES * EDGE_ROWS
 SENT = RELAY_AT + 2 * RELAY_ROWS
 GHOST = SENT + 32
-SMALL = GHOST - EDGE_AT
 SHARE = 384
+COLUMNS = WIDE + GHOST
+NONE = LANES - 1
 HELD = ((-1, 0, 0), (1, 0, 0), (0, 0, -1), (0, 0, 1), (-1, 0, -1), (-1, 0, 1), (1, 0, -1), (1, 0, 1))
 
 
@@ -92,6 +93,27 @@
     return picks
 
 
+def column_slots():
+    slots = np.full((1, COLUMNS), -1.0, np.float32)
+    orbitals = np.zeros((1, COLUMNS), np.int32)
+    for b in range(ORB):
+        slots[0, b * LANES : (b + 1) * LANES] = np.arange(LANES)
+        orbitals[0, b * LANES : (b + 1) * LANES] = b
+        for f in range(FACES):
+            at = WIDE + (f * ORB + b) * FACE
+            slots[0, at : at + FACE] = LANES + f * FACE + np.arange(FACE)
+            orbitals[0, at : at + FACE] = b
+        for e in range(EDGES):
+            at = WIDE + EDGE_AT + e * EDGE_ROWS + b * EDGE
+            slots[0, at : at + EDGE] = LANES + FACES * FACE + e * EDGE + np.arange(EDGE)
+            orbitals[0, at : at + EDGE] = b
+        for side in range(2):
+            at = WIDE + RELAY_AT + side * RELAY_ROWS + b * RELAY
+            slots[0, at : at + RELAY] = LANES + DIRECT + side * RELAY + np.arange(RELAY)
+            orbitals[0, at : at + RELAY] = b
+    return slots, orbitals * (NEIGH - 1)
+
+
 def segment_spans():
     spans = np.zeros((COPIES, 8, SHARE), np.float32)
     for at, (_, first, count) in enumerate(SEGMENTS):
@@ -122,25 +144,25 @@
     picks,
     relays,
     spans,
+    column_slot,
+    column_base,
     w_out,
     f_out,
-    ht_own,
-    ht_ghost,
+    operator,
+    lookup,
+    table,
     onehot,
     ext_own,
-    ext_ghost,
     noise_ext,
     gathered,
     chain,
     res,
+    res_t,
     acc,
     sbuf,
     rbuf,
     small,
-    small_ham,
     small_relay,
-    near_slot,
-    far_slot,
     fsend,
     frecv,
     pairs,
@@ -226,7 +248,6 @@
             copy.start()
 
     small[...] = jnp.zeros(small.shape, f32)
-    small_ham[...] = jnp.zeros(small_ham.shape, f32)
     small_relay[...] = jnp.zeros(small_relay.shape, f32)
     for step in range(5):
         rbuf[step, SENT:GHOST] = jnp.zeros((GHOST - SENT, LANES), bf16)
@@ -234,12 +255,6 @@
     pl.semaphore_wait(barrier, COPIES)
     for copy in flying[0]:
         copy.start()
-
-    for b in range(ORB):
-        turned = noise[b].astype(f32).T
-        chain[0, :, b * LANES : (b + 1) * LANES] = turned
-        ext_own[0:LANES, b * LANES : (b + 1) * LANES] = turned.astype(bf16)
-        noise_ext[b * LANES : (b + 1) * LANES, 0:LANES] = turned.astype(bf16)
 
     @pl.loop(0, EXT // LANES)
     def _(part):
@@ -251,126 +266,126 @@
                 same, 1.0, 0.0
             ).astype(bf16)
 
-    @pl.loop(0, (LANES + PICKED) // 8)
+    turned = jnp.concatenate([index[...], index[0:1]], axis=0).astype(f32).T
+    res[0:LANES, 0:16] = turned
+
+    @pl.loop(0, LANES // 8)
     def _(part):
-        first = pl.multiple_of(part * 8, 8)
-        rows = lax.broadcasted_iota(jnp.int32, (8, LANES), 0) + first
-        for found, low in ((near_slot, 1), (far_slot, 8)):
-            which = jnp.full((8, LANES), 7, jnp.int32)
-            for at in range(7):
-                which = jnp.where(rows == index[low + at : low + at + 1, :], at, which)
-            found[pl.ds(first, 8)] = which
-
-    def fill_columns(a):
-        columns = pl.ds(pl.multiple_of(a * LANES, LANES), LANES)
-        last = lax.broadcasted_iota(jnp.int32, (8, LANES), 0) == 7
-        for b in range(ORB):
-            blocks = ham[a, b].astype(f32)
-            itself = blocks[0:1]
-            tables = []
-            for low in (1, 8):
-                rows = jnp.concatenate([blocks[low : low + 7], blocks[0:1]], axis=0)
-                tables.append(jnp.where(last, 0.0, rows))
-
-            def block(first, count):
+        lines = pl.ds(pl.multiple_of(part * 8, 8), 8)
+        near = res[lines, 0:16]
+        near = [jnp.broadcast_to(near[:, m : m + 1], (8, LANES)) for m in range(1, NEIGH)]
+        own = None
+        for tile in range(COLUMNS // LANES):
+            cut = slice(tile * LANES, (tile + 1) * LANES)
+            base = column_base[0:1, cut]
+            if 0 < tile < ORB:
+                which = jnp.where(own == NONE, NONE, own + tile * (NEIGH - 1))
+            else:
+                slot = column_slot[0:1, cut]
+                which = jnp.full((8, LANES), NONE, jnp.int32)
+                for m in range(NEIGH - 1):
+                    which = jnp.where(near[m] == slot, base + m, which)
+                if tile == 0:
+                    own = which
+            lookup[lines, cut] = which
+
+    def fill_rows(a):
+        blocks = [ham[a, b].astype(f32) for b in range(ORB)]
+        lines = [block[1:NEIGH] for block in blocks]
+        lines.append(jnp.zeros((LANES - ORB * (NEIGH - 1), LANES), f32))
+        table[:, 0:LANES] = jnp.concatenate(lines, axis=0).T
+        firsts = [block[0:1] for block in blocks] + [jnp.zeros((16 - ORB, LANES), f32)]
+        table[:, LANES : LANES + 16] = jnp.concatenate(firsts, axis=0).T
+        shape = (8, LANES)
+        for pair in range(LANES // 16):
+            at = pl.multiple_of(a * LANES + pair * 16, 16)
+            for tile in range(COLUMNS // LANES):
+                cut = slice(tile * LANES, (tile + 1) * LANES)
                 made = []
-                for at in range(first, first + count, 8):
-                    made.append(
-                        jnp.take_along_axis(tables[0], near_slot[at : at + 8], axis=0)
-                        + jnp.take_along_axis(tables[1], far_slot[at : at + 8], axis=0)
+                for low in (pair * 16, pair * 16 + 8):
+                    found = jnp.take_along_axis(
+                        table[low : low + 8, 0:LANES], lookup[low : low + 8, cut], axis=1
                     )
-                return jnp.concatenate(made, axis=0)
-
-            own = block(0, LANES)
-            shape = (LANES, LANES)
-            same = lax.broadcasted_iota(jnp.int32, shape, 0) == lax.broadcasted_iota(
-                jnp.int32, shape, 1
-            )
-            own = jnp.where(same, itself, own)
-            ht_own[b * LANES : (b + 1) * LANES, columns] = own.astype(bf16)
-            for f in range(FACES):
-                to = (f * ORB + b) * FACE
-                made = block(LANES + f * FACE, FACE)
-                ht_ghost[to : to + FACE, columns] = made.astype(bf16)
-            for e in range(EDGES):
-                to = e * EDGE_ROWS + b * EDGE
-                small_ham[to : to + EDGE] = block(LANES + FACES * FACE + e * EDGE, EDGE)
-            for side in range(2):
-                to = RELAY_AT - EDGE_AT + side * RELAY_ROWS + b * RELAY
-                small_ham[to : to + RELAY] = block(LANES + DIRECT + side * RELAY, RELAY)
-        ht_ghost[EDGE_AT:GHOST, columns] = small_ham[...].astype(bf16)
-
-    pl.loop(0, 5)(fill_columns)
+                    if tile < ORB:
+                        itself = table[low : low + 8, LANES + tile : LANES + tile + 1]
+                        same = lax.broadcasted_iota(jnp.int32, shape, 0) + low
+                        same = same == lax.broadcasted_iota(jnp.int32, shape, 1)
+                        found = jnp.where(same, itself, found)
+                    made.append(found)
+                operator[pl.ds(at, 16), cut] = jnp.concatenate(made, axis=0).astype(bf16)
+
+    pl.loop(0, 5)(fill_rows)
     pass_on(0)
-    pl.loop(5, ORB)(fill_columns)
-
-    def multiply(rows, ext, operator, first, span=slice(None)):
-        @pl.loop(0, 3)
-        def _(part):
-            columns = pl.ds(pl.multiple_of(part * SHARE, SHARE), SHARE)
-            product = dot(ext[rows, span], operator[span, columns])
-            if first:
-                acc[rows, columns] = product
-            else:
-                acc[rows, columns] += product
-
-    def multiply_ghosts(step, rows):
+    pl.loop(5, ORB)(fill_rows)
+
+    own_columns = slice(0, WIDE)
+    direct_columns = slice(WIDE, WIDE + RELAY_AT)
+    relay_columns = slice(WIDE + RELAY_AT, COLUMNS)
+
+    def multiply_ghosts(step, half):
         if step > 0:
             pass_on(step)
-        ext_ghost[rows, 0:RELAY_AT] = rbuf[step, 0:RELAY_AT].T
-        multiply(rows, ext_ghost, ht_ghost, False, slice(0, RELAY_AT))
+        acc[half] += dot(operator[:, direct_columns], rbuf[step, 0:RELAY_AT])
         for copy in relayed[step]:
             copy.wait_recv()
-        ext_ghost[rows, RELAY_AT:GHOST] = rbuf[step, RELAY_AT:GHOST].T
-        multiply(rows, ext_ghost, ht_ghost, False, slice(RELAY_AT, GHOST))
-
-    vectors = (slice(0, HALF), slice(HALF, LANES))
-    pieces = (slice(0, LANES), slice(LANES, 2 * LANES))
+        acc[half] += dot(operator[:, relay_columns], rbuf[step, RELAY_AT:GHOST])
+
+    left = lax.broadcasted_iota(jnp.int32, (WIDE, LANES), 1) < HALF
 
     def summed(half):
-        base = half * LANES
-        return acc[base : base + HALF] + acc[base + HALF : base + LANES]
+        return acc[half] + pltpu.roll(acc[half], HALF, 1)
 
     def send_half(order, half):
-        high, low = halves(chain[order, vectors[half]])
-        ext_own[half * LANES : half * LANES + HALF] = high
-        ext_own[half * LANES + HALF : (half + 1) * LANES] = low
+        value = chain[order]
+        high = value.astype(bf16).astype(f32)
+        low = value - high
+        if half == 0:
+            both = jnp.where(left, high, pltpu.roll(low, HALF, 1))
+        else:
+            both = jnp.where(left, pltpu.roll(high, HALF, 1), low)
+        ext_own[:, half * LANES : (half + 1) * LANES] = both.astype(bf16)
         step = 2 * order - 1 + half
         pack(
             step,
-            lambda b: dot_t(picks[0:DIRECT], ext_own[pieces[half], b * LANES : (b + 1) * LANES]),
+            lambda b: dot(
+                picks[0:DIRECT],
+                ext_own[b * LANES : (b + 1) * LANES, half * LANES : (half + 1) * LANES],
+            ),
         )
         for copy in flying[step]:
             copy.start()
 
-    multiply(pieces[0], ext_own, ht_own, True)
-    multiply_ghosts(0, pieces[0])
-    chain[1] = acc[0:LANES]
+    for b in range(ORB):
+        chain[0, b * LANES : (b + 1) * LANES] = noise[b].astype(f32)
+        ext_own[b * LANES : (b + 1) * LANES, 0:LANES] = noise[b]
+    acc[0] = dot(operator[:, own_columns], ext_own[:, 0:LANES])
+    multiply_ghosts(0, 0)
+    chain[1] = acc[0]
     send_half(1, 0)
     send_half(1, 1)
     res[...] = coef[0] * chain[0] + coef[1] * chain[1]
 
+    both = dot(operator[:, own_columns], ext_own[...])
+    acc[0] = both[:, 0:LANES]
+    acc[1] = both[:, LANES:]
+    small_ghost = rbuf[0, EDGE_AT:GHOST].astype(f32)
     for b in range(ORB):
         parts = []
         for f in range(FACES):
             at = (f * ORB + b) * FACE
             parts.append(rbuf[0, at : at + FACE])
-        noise_rows = jnp.concatenate(parts, axis=0)
-        noise_ext[b * LANES : (b + 1) * LANES, LANES : LANES + FACES * FACE] = noise_rows.T
-    small_ghost = rbuf[0, EDGE_AT:GHOST].astype(f32)
-    for b in range(ORB):
-        parts = []
+        lines = []
         for e in range(EDGES):
             at = e * EDGE_ROWS + b * EDGE
-            parts.append(small_ghost[at : at + EDGE])
+            lines.append(small_ghost[at : at + EDGE])
         for side in range(2):
             at = RELAY_AT - EDGE_AT + side * RELAY_ROWS + b * RELAY
-            parts.append(small_ghost[at : at + RELAY])
-        parts.append(jnp.zeros((EXT - LANES - PICKED, LANES), f32))
-        noise_rows = jnp.concatenate(parts, axis=0).astype(bf16)
-        noise_ext[b * LANES : (b + 1) * LANES, LANES + FACES * FACE : EXT] = noise_rows.T
-
-    multiply(slice(0, 2 * LANES), ext_own, ht_own, True)
+            lines.append(small_ghost[at : at + RELAY])
+        lines.append(jnp.zeros((EXT - LANES - PICKED, LANES), f32))
+        parts.append(jnp.concatenate(lines, axis=0).astype(bf16))
+        cut = slice(b * LANES, (b + 1) * LANES)
+        noise_ext[cut, 0:LANES] = noise[b].T
+        noise_ext[cut, LANES:EXT] = jnp.concatenate(parts, axis=0).T
 
     @pl.loop(0, (NEIGH - 1) // 2)
     def _(two):
@@ -380,17 +395,22 @@
         gathered[2 * two + 1] = both[:, LANES:]
 
     for half in range(2):
-        multiply_ghosts(1 + half, pieces[half])
-        chain[2, vectors[half]] = 2.0 * summed(half) - chain[0, vectors[half]]
+        multiply_ghosts(1 + half, half)
+        fresh = 2.0 * summed(half) - chain[0]
+        chain[2] = fresh if half == 0 else jnp.where(left, chain[2], fresh)
         send_half(2, half)
-        multiply(pieces[half], ext_own, ht_own, True)
+        cut = slice(half * LANES, (half + 1) * LANES)
+        acc[half] = dot(operator[:, own_columns], ext_own[:, cut])
     res[...] += coef[2] * chain[2]
 
     dens[:, 0:1] = jnp.zeros((ORB * ORB, 1, LANES), f32)
 
     for half in range(2):
-        multiply_ghosts(3 + half, pieces[half])
-        res[vectors[half]] += coef[3] * (2.0 * summed(half) - chain[1, vectors[half]])
+        multiply_ghosts(3 + half, half)
+        fresh = coef[3] * (2.0 * summed(half) - chain[1])
+        res[...] += jnp.where(left, fresh, 0.0) if half == 0 else jnp.where(left, 0.0, fresh)
+        for a in range(ORB):
+            res_t[a] = res[a * LANES : (a + 1) * LANES].T
 
         @pl.loop(1, NEIGH)
         def _(m):
@@ -398,7 +418,7 @@
                 base = b * LANES + half * HALF
                 near = gathered[m - 1, base : base + HALF].astype(f32)
                 for a in range(ORB):
-                    term = res[vectors[half], a * LANES : (a + 1) * LANES] * near
+                    term = res_t[a, half * HALF : (half + 1) * HALF] * near
                     row = jnp.sum(term, axis=0, keepdims=True)
                     if half == 0:
                         dens[a * ORB + b, pl.ds(m, 1)] = row
@@ -441,7 +461,7 @@
     for copy in back:
         copy.start()
     for a in range(ORB):
-        w_out[a] = res[:, a * LANES : (a + 1) * LANES].T
+        w_out[a] = res[a * LANES : (a + 1) * LANES]
     for copy in back:
         copy.wait_recv()
     total = spread[:, 0:LANES]
@@ -492,6 +512,7 @@
     picks = jnp.asarray(picking_matrix(), bf16)
     relays = jnp.asarray(relaying_matrix(), bf16)
     spans = jnp.asarray(segment_spans(), f32)
+    column_slot, column_base = (jnp.asarray(value) for value in column_slots())
     vmem = pl.BlockSpec(memory_space=pltpu.VMEM)
     smem = pl.BlockSpec(memory_space=pltpu.SMEM)
     return pl.pallas_call(
@@ -500,26 +521,24 @@
             jax.ShapeDtypeStruct((ORB, LANES, LANES), f32),
             jax.ShapeDtypeStruct((3, LANES), f32),
         ),
-        in_specs=[vmem, vmem, vmem, vmem, smem, vmem, vmem, vmem],
+        in_specs=[vmem, vmem, vmem, vmem, smem, vmem, vmem, vmem, vmem, vmem],
         out_specs=(vmem, vmem),
         scratch_shapes=[
-            pltpu.VMEM((WIDE, WIDE), bf16),
-            pltpu.VMEM((GHOST, WIDE), bf16),
+            pltpu.VMEM((WIDE, COLUMNS), bf16),
+            pltpu.VMEM((LANES, COLUMNS), jnp.int32),
+            pltpu.VMEM((LANES, 2 * LANES), f32),
             pltpu.VMEM((EXT, NEIGH * LANES), bf16),
-            pltpu.VMEM((2 * LANES, WIDE), bf16),
-            pltpu.VMEM((2 * LANES, GHOST), bf16),
+            pltpu.VMEM((WIDE, 2 * LANES), bf16),
             pltpu.VMEM((WIDE, EXT), bf16),
             pltpu.VMEM((NEIGH - 1, WIDE, LANES), bf16),
-            pltpu.VMEM((3, LANES, WIDE), f32),
-            pltpu.VMEM((LANES, WIDE), f32),
-            pltpu.VMEM((2 * LANES, WIDE), f32),
+            pltpu.VMEM((3, WIDE, LANES), f32),
+            pltpu.VMEM((WIDE, LANES), f32),
+            pltpu.VMEM((ORB, LANES, LANES), f32),
+            pltpu.VMEM((2, WIDE, LANES), f32),
             pltpu.VMEM((5, SENT, LANES), bf16),
             pltpu.VMEM((5, GHOST, LANES), bf16),
             pltpu.VMEM((EDGES * EDGE_ROWS, LANES), f32),
-            pltpu.VMEM((SMALL, LANES), f32),
             pltpu.VMEM((2 * RELAY_ROWS, LANES), f32),
-            pltpu.VMEM((LANES + PICKED, LANES), jnp.int32),
-            pltpu.VMEM((LANES + PICKED, LANES), jnp.int32),
             pltpu.VMEM((COPIES, 8, LANES), f32),
             pltpu.VMEM((COPIES, 8, LANES), f32),
             pltpu.VMEM((8, NEIGH * LANES), f32),
@@ -531,7 +550,7 @@
             collective_id=0, has_side_effects=True, vmem_limit_bytes=56 * 1024 * 1024
         ),
         name="fermi_forces",
-    )(noise, ham, deriv, index, coef, picks, relays, spans)
+    )(noise, ham, deriv, index, coef, picks, relays, spans, column_slot, column_base)
 
 
 def solution(mesh):

time: 76.5 us -> 87.3 us (1.14)
  Pallas kernels: 71.8 us -> 82.6 us
    pallas_call x1, Pallas kernels: 71.8 us -> 82.6 us  [shards(): pl.pallas_call(functools.partial(kernel, sizes), out_shape=(jax.ShapeDtyp...]
where the time goes in v3:
time: 87.3 us; the launch traced here: 87.1 us
  Pallas kernels  82.6 us (95%)
  local copies, waits for them, and re-layouts  3.19 us (4%)
    pallas_call x1, Pallas kernels, shards(): pl.pallas_call(functools.partial(kernel, sizes), out_shape=(jax.ShapeDtyp...  82.6 us
    unnamed x6, local copies, waits for them, and re-layouts  3.19 us

profile of v3, /device:TPU:0, one launch (start us, length us, event | category | flops | bytes accessed | tf_op | source)
XLA Modules:
  0.0 87.1 jit_solution(6360708265317035545)
XLA Ops:
  0.6 0.0 copy-start
  0.6 0.7 copy-done
  1.3 0.7 select_add_fusion.index
  2.0 82.6 %fermi_forces.1 = (f32[9,128,128]{2,1,0:T(8,128)}, f32[3,128]{1,0:T(4,128)}) custom-call(bf16[9,128,128]{2,1,0:T(8,128)(2,1)} %noise.1, bf16[9,9,15,128]{3,2,1,0:T(8,128)(2,1)} %bitcast.23, bf16[3,81,15,128]{3,2,1,0:T(8,128)(2,1)} %bitcast.22, s32[15,128]{1,0:T(8,128)} %select_add_fusion.index, f32[4]{0:T(128)} %coef.1, ...), custom_call_target="tpu_custom_call" | custom-call | tf_op jit(solution)/shard_map/fermi_forces/pallas_call | solution.py:518
  84.6 0.0 copy-start.1
  84.6 1.9 %copy.14 = f32[9,128,128]{2,1,0:T(8,128)} copy(f32[9,128,128]{2,1,0:T(8,128)} %get-tuple-element.4) | data formatting | bytes 1179648
  86.6 0.0 copy-done.1
  86.6 0.6 copy.15
Async XLA Ops:
  0.6 0.7 copy-start
  84.6 1.9 %copy-start.1 = (f32[3,128]{1,0:T(4,128)S(1)}, f32[3,128]{1,0:T(4,128)}, u32[]{:S(2)}) copy-start(f32[3,128]{1,0:T(4,128)} %get-tuple-element.5) | copy-start | bytes 4612

commit v4 on v2

--- a/solution.py
+++ b/solution.py
@@ -264,7 +264,8 @@
     def fill_columns(a):
         columns = pl.ds(pl.multiple_of(a * LANES, LANES), LANES)
         last = lax.broadcasted_iota(jnp.int32, (8, LANES), 0) == 7
-        for b in range(ORB):
+
+        def fill_block(b):
             blocks = ham[a, b].astype(f32)
             itself = blocks[0:1]
             tables = []
@@ -287,17 +288,23 @@
                 jnp.int32, shape, 1
             )
             own = jnp.where(same, itself, own)
-            ht_own[b * LANES : (b + 1) * LANES, columns] = own.astype(bf16)
+            ht_own[pl.ds(pl.multiple_of(b * LANES, LANES), LANES), columns] = own.astype(bf16)
             for f in range(FACES):
-                to = (f * ORB + b) * FACE
+                to = pl.multiple_of((f * ORB + b) * FACE, FACE)
                 made = block(LANES + f * FACE, FACE)
-                ht_ghost[to : to + FACE, columns] = made.astype(bf16)
+                ht_ghost[pl.ds(to, FACE), columns] = made.astype(bf16)
             for e in range(EDGES):
-                to = e * EDGE_ROWS + b * EDGE
-                small_ham[to : to + EDGE] = block(LANES + FACES * FACE + e * EDGE, EDGE)
+                to = pl.multiple_of(e * EDGE_ROWS + b * EDGE, EDGE)
+                small_ham[pl.ds(to, EDGE)] = block(LANES + FACES * FACE + e * EDGE, EDGE)
             for side in range(2):
-                to = RELAY_AT - EDGE_AT + side * RELAY_ROWS + b * RELAY
-                small_ham[to : to + RELAY] = block(LANES + DIRECT + side * RELAY, RELAY)
+                to = pl.multiple_of(RELAY_AT - EDGE_AT + side * RELAY_ROWS + b * RELAY, 8)
+                small_ham[pl.ds(to, RELAY)] = block(LANES + DIRECT + side * RELAY, RELAY)
+
+        @pl.loop(0, ORB // 3)
+        def _(group):
+            for at in range(3):
+                fill_block(group * 3 + at)
+
         ht_ghost[EDGE_AT:GHOST, columns] = small_ham[...].astype(bf16)
 
     pl.loop(0, 5)(fill_columns)
@@ -305,14 +312,18 @@
     pl.loop(5, ORB)(fill_columns)
 
     def multiply(rows, ext, operator, first, span=slice(None)):
-        @pl.loop(0, 3)
-        def _(part):
-            columns = pl.ds(pl.multiple_of(part * SHARE, SHARE), SHARE)
+        def share(columns):
             product = dot(ext[rows, span], operator[span, columns])
             if first:
                 acc[rows, columns] = product
             else:
                 acc[rows, columns] += product
+
+        @pl.loop(0, 2)
+        def _(part):
+            share(pl.ds(pl.multiple_of(part * 4 * LANES, 4 * LANES), 4 * LANES))
+
+        share(slice(8 * LANES, WIDE))
 
     def multiply_ghosts(step, rows):
         if step > 0:
@@ -394,16 +405,19 @@
 
         @pl.loop(1, NEIGH)
         def _(m):
-            for b in range(ORB):
-                base = b * LANES + half * HALF
-                near = gathered[m - 1, base : base + HALF].astype(f32)
-                for a in range(ORB):
-                    term = res[vectors[half], a * LANES : (a + 1) * LANES] * near
-                    row = jnp.sum(term, axis=0, keepdims=True)
-                    if half == 0:
-                        dens[a * ORB + b, pl.ds(m, 1)] = row
-                    else:
-                        dens[a * ORB + b, pl.ds(m, 1)] += row
+            @pl.loop(0, ORB // 3)
+            def _(group):
+                for at in range(3):
+                    b = group * 3 + at
+                    base = pl.multiple_of(b * LANES + half * HALF, HALF)
+                    near = gathered[m - 1, pl.ds(base, HALF)].astype(f32)
+                    for a in range(ORB):
+                        term = res[vectors[half], a * LANES : (a + 1) * LANES] * near
+                        row = jnp.sum(term, axis=0, keepdims=True)
+                        if half == 0:
+                            dens[a * ORB + b, pl.ds(m, 1)] = row
+                        else:
+                            dens[a * ORB + b, pl.ds(m, 1)] += row
 
     pairs[...] = jnp.zeros(pairs.shape, f32)
     for c in range(3):
@@ -416,7 +430,7 @@
         for m in range(1, NEIGH):
             pairs[c : c + 1, m * LANES : (m + 1) * LANES] = pair[m : m + 1]
     high, low = halves(pairs[...])
-    spread = dot_t(jnp.concatenate([high, low], axis=0), onehot[...])
+    spread = dot_t(onehot[...], jnp.concatenate([high, low], axis=0)).T
     spread = spread[0:8] + spread[8:16]
     high, low = halves(spread[:, LANES:EXT])
     mask = spans[...]

time: 76.5 us -> 76.3 us (level)
  no operation moved by 1% of the time
where the time goes in v4:
time: 76.3 us; the launch traced here: 76.1 us
  Pallas kernels  71.5 us (94%)
  local copies, waits for them, and re-layouts  3.19 us (4%)
    pallas_call x1, Pallas kernels, shards(): pl.pallas_call(functools.partial(kernel, sizes), out_shape=(jax.ShapeDtyp...  71.5 us
    unnamed x6, local copies, waits for them, and re-layouts  3.19 us

profile of v4, /device:TPU:0, one launch (start us, length us, event | category | flops | bytes accessed | tf_op | source)
XLA Modules:
  0.0 76.1 jit_solution(10208466003562121285)
XLA Ops:
  0.6 0.0 copy-start
  0.6 0.7 copy-done
  1.3 0.7 select_add_fusion.index
  2.0 71.5 %fermi_forces.1 = (f32[9,128,128]{2,1,0:T(8,128)}, f32[3,128]{1,0:T(4,128)}) custom-call(bf16[9,128,128]{2,1,0:T(8,128)(2,1)} %noise.1, bf16[9,9,15,128]{3,2,1,0:T(8,128)(2,1)} %bitcast.23, bf16[3,81,15,128]{3,2,1,0:T(8,128)(2,1)} %bitcast.22, s32[15,128]{1,0:T(8,128)} %select_add_fusion.index, f32[4]{0:T(128)} %coef.1, ...), custom_call_target="tpu_custom_call" | custom-call | tf_op jit(solution)/shard_map/fermi_forces/pallas_call | solution.py:511
  73.5 0.0 copy-start.1
  73.6 1.9 %copy.12 = f32[9,128,128]{2,1,0:T(8,128)} copy(f32[9,128,128]{2,1,0:T(8,128)} %get-tuple-element.4) | data formatting | bytes 1179648
  75.5 0.0 copy-done.1
  75.5 0.6 copy.13
Async XLA Ops:
  0.6 0.7 copy-start
  73.5 1.9 %copy-start.1 = (f32[3,128]{1,0:T(4,128)S(1)}, f32[3,128]{1,0:T(4,128)}, u32[]{:S(2)}) copy-start(f32[3,128]{1,0:T(4,128)} %get-tuple-element.5) | copy-start | bytes 4612

commit v5 on v4

--- a/solution.py
+++ b/solution.py
@@ -326,8 +326,6 @@
         share(slice(8 * LANES, WIDE))
 
     def multiply_ghosts(step, rows):
-        if step > 0:
-            pass_on(step)
         ext_ghost[rows, 0:RELAY_AT] = rbuf[step, 0:RELAY_AT].T
         multiply(rows, ext_ghost, ht_ghost, False, slice(0, RELAY_AT))
         for copy in relayed[step]:
@@ -383,17 +381,21 @@
 
     multiply(slice(0, 2 * LANES), ext_own, ht_own, True)
 
-    @pl.loop(0, (NEIGH - 1) // 2)
-    def _(two):
+    def gather(two):
         hot = onehot[:, pl.ds(pl.multiple_of(two * 2 * LANES + LANES, LANES), 2 * LANES)]
         both = dot(noise_ext[...], hot).astype(bf16)
         gathered[2 * two] = both[:, 0:LANES]
         gathered[2 * two + 1] = both[:, LANES:]
 
+    pl.loop(0, 3)(gather)
+    pass_on(1)
+    pl.loop(3, (NEIGH - 1) // 2)(gather)
+
     for half in range(2):
         multiply_ghosts(1 + half, pieces[half])
         chain[2, vectors[half]] = 2.0 * summed(half) - chain[0, vectors[half]]
         send_half(2, half)
+        pass_on(2 + half)
         multiply(pieces[half], ext_own, ht_own, True)
     res[...] += coef[2] * chain[2]
 
@@ -403,8 +405,7 @@
         multiply_ghosts(3 + half, pieces[half])
         res[vectors[half]] += coef[3] * (2.0 * summed(half) - chain[1, vectors[half]])
 
-        @pl.loop(1, NEIGH)
-        def _(m):
+        def densities(m):
             @pl.loop(0, ORB // 3)
             def _(group):
                 for at in range(3):
@@ -418,6 +419,13 @@
                             dens[a * ORB + b, pl.ds(m, 1)] = row
                         else:
                             dens[a * ORB + b, pl.ds(m, 1)] += row
+
+        if half == 0:
+            pl.loop(1, 8)(densities)
+            pass_on(4)
+            pl.loop(8, NEIGH)(densities)
+        else:
+            pl.loop(1, NEIGH)(densities)
 
     pairs[...] = jnp.zeros(pairs.shape, f32)
     for c in range(3):

time: 76.3 us -> 75.4 us (0.988)
  Pallas kernels: 71.5 us -> 70.7 us
    pallas_call x1, Pallas kernels: 71.5 us -> 70.7 us  [shards(): pl.pallas_call(functools.partial(kernel, sizes), out_shape=(jax.ShapeDtyp...]
where the time goes in v5:
time: 75.4 us; the launch traced here: 75.2 us
  Pallas kernels  70.7 us (94%)
  local copies, waits for them, and re-layouts  3.19 us (4%)
    pallas_call x1, Pallas kernels, shards(): pl.pallas_call(functools.partial(kernel, sizes), out_shape=(jax.ShapeDtyp...  70.7 us
    unnamed x6, local copies, waits for them, and re-layouts  3.19 us

profile of v5, /device:TPU:0, one launch (start us, length us, event | category | flops | bytes accessed | tf_op | source)
XLA Modules:
  0.0 75.2 jit_solution(8887821942076875402)
XLA Ops:
  0.6 0.0 copy-start
  0.6 0.7 copy-done
  1.3 0.7 select_add_fusion.index
  2.0 70.7 %fermi_forces.1 = (f32[9,128,128]{2,1,0:T(8,128)}, f32[3,128]{1,0:T(4,128)}) custom-call(bf16[9,128,128]{2,1,0:T(8,128)(2,1)} %noise.1, bf16[9,9,15,128]{3,2,1,0:T(8,128)(2,1)} %bitcast.23, bf16[3,81,15,128]{3,2,1,0:T(8,128)(2,1)} %bitcast.22, s32[15,128]{1,0:T(8,128)} %select_add_fusion.index, f32[4]{0:T(128)} %coef.1, ...), custom_call_target="tpu_custom_call" | custom-call | tf_op jit(solution)/shard_map/fermi_forces/pallas_call | solution.py:519
  72.7 0.0 copy-start.1
  72.7 1.9 %copy.12 = f32[9,128,128]{2,1,0:T(8,128)} copy(f32[9,128,128]{2,1,0:T(8,128)} %get-tuple-element.4) | data formatting | bytes 1179648
  74.6 0.0 copy-done.1
  74.6 0.6 copy.13
Async XLA Ops:
  0.6 0.7 copy-start
  72.7 1.9 %copy-start.1 = (f32[3,128]{1,0:T(4,128)S(1)}, f32[3,128]{1,0:T(4,128)}, u32[]{:S(2)}) copy-start(f32[3,128]{1,0:T(4,128)} %get-tuple-element.5) | copy-start | bytes 4612
